TPU v7x, 32 devices: a whole 2x2x4 slice. The times are simulated.
32 devices in a mesh: dp: 4 (over z), section: 4 (over x, core), mp: 2 (over y).
Axes of the slice: x: 2, y: 2, z: 4, core: 2. Of those that a mesh axis runs over, the one named last changes fastest.
Arguments:
- arriving: bfloat16 [4, 576, 8192], P('section', 'dp', 'mp'), may hold values from -6 to 6
- keep_mask: int32 [576], P('dp'), may hold values 0 or 1
- mask_vector: bfloat16 [8192], P('mp'), may hold values from -5 to 5
- stashed: bfloat16 [4, 576, 8192], P('section', 'dp', 'mp'), may hold values from -6 to 6
- cotangent: bfloat16 [4, 576, 8192], P('section', 'dp', 'mp'), may hold values from -6 to 6
- gain: bfloat16 [4, 8192], P('section', 'mp'), may hold values from 0.3984375 to 1.59375
- down_adapter: bfloat16 [4, 8192, 256], P('section', None, 'mp'), may hold values from -0.0625 to 0.0625
- up_adapter: bfloat16 [4, 256, 8192], P('section', 'mp'), may hold values from -0.375 to 0.375
Outputs:
- next_input: bfloat16 [4, 576, 8192], P('section', 'dp', 'mp')
- prev_grad: bfloat16 [4, 576, 8192], P('section', 'dp', 'mp')
- down_grad: float32 [4, 8192, 256], P('section', 'dp', 'mp')
- up_grad: float32 [4, 256, 8192], P('section', 'mp', 'dp')
All inputs are finite; a program needn't handle non-finite values. No bound on the sum of `keep_mask` on one device may be relied on, other than what follows from the above.
Results may differ from a plain program's by a relative error of at most 0.0015.
The roundings to bfloat16 on the way count: a program that leaves them out, or rounds other values in their place, can miss the bound.
Values may be sent and summed in bfloat16 or wider, within the bound.
A program may use at most 128 MiB of HBM per device.

v0:
```python
import jax
import jax.numpy as jnp
from jax import lax
from jax.sharding import PartitionSpec as P


def shifted(shard, axis, by):
    peers = lax.axis_size(axis)
    pairs = [(i, i + by) for i in range(peers) if 0 <= i + by < peers]
    return lax.ppermute(shard, axis, pairs)


def row_scale(rows):
    values = rows.astype(jnp.float32)
    return lax.rsqrt(jnp.mean(values * values, axis=1, keepdims=True) + 1e-05)


def contract_rows(left, right):
    return lax.dot_general(
        left, right, (((0,), (0,)), ((), ())), preferred_element_type=jnp.float32
    )


def contract_cols(left, right):
    return lax.dot_general(
        left, right, (((1,), (1,)), ((), ())), preferred_element_type=jnp.float32
    )


def on_device(arriving, keep_mask, mask_vector, stashed, cotangent, gain, down_adapter, up_adapter):
    is_first = lax.axis_index("section") == 0
    kept_rows = jnp.logical_or(keep_mask == 1, jnp.logical_not(is_first))
    inputs = jnp.where(kept_rows[:, None], arriving[0], mask_vector[None, :])
    saved = stashed[0]
    upstream = cotangent[0]
    gain_part = gain[0]
    down_local = down_adapter[0]
    up_local = up_adapter[0]
    replicas = lax.axis_size("dp")
    inputs_full, saved_full, upstream_full, gain_full = (
        lax.all_gather(inputs, "mp", axis=1, tiled=True),
        lax.all_gather(saved, "mp", axis=1, tiled=True),
        lax.all_gather(upstream, "mp", axis=1, tiled=True),
        lax.all_gather(gain_part, "mp", axis=0, tiled=True),
    )
    gain_row = gain_full.astype(jnp.float32)[None, :]
    full_width = inputs_full.shape[1]
    normed = (inputs_full.astype(jnp.float32) * row_scale(inputs_full) * gain_row).astype(
        jnp.bfloat16
    )
    hidden_pre = jnp.dot(normed, down_local, preferred_element_type=jnp.float32)
    hidden = jax.nn.silu(hidden_pre).astype(jnp.bfloat16)
    branch_part = jnp.dot(hidden, up_local, preferred_element_type=jnp.float32)
    saved_scale = row_scale(saved_full)
    saved_normed = (saved_full.astype(jnp.float32) * saved_scale * gain_row).astype(jnp.bfloat16)
    saved_pre = jnp.dot(saved_normed, down_local, preferred_element_type=jnp.float32)
    sigmoid_pre = jax.nn.sigmoid(saved_pre)
    saved_hidden = (saved_pre * sigmoid_pre).astype(jnp.bfloat16)
    hidden_grad = contract_cols(upstream_full, up_local)
    pre_grad = (hidden_grad * sigmoid_pre * (1.0 + saved_pre * (1.0 - sigmoid_pre))).astype(
        jnp.bfloat16
    )
    normed_part = contract_cols(pre_grad, down_local)
    down_part = contract_rows(saved_normed, pre_grad)
    up_part = contract_rows(saved_hidden, upstream_full)
    down_sum, up_sum = (
        lax.psum_scatter(down_part, "dp", scatter_dimension=0, tiled=True),
        lax.psum_scatter(up_part, "dp", scatter_dimension=1, tiled=True),
    )
    branch, normed_grad = (
        lax.psum_scatter(branch_part, "mp", scatter_dimension=1, tiled=True),
        lax.psum_scatter(normed_part, "mp", scatter_dimension=1, tiled=True),
    )
    output = (inputs.astype(jnp.float32) + branch).astype(jnp.bfloat16)
    saved_values = saved.astype(jnp.float32)
    scaled_grad = normed_grad * gain_part.astype(jnp.float32)[None, :]
    row_dot = lax.psum(jnp.sum(saved_values * scaled_grad, axis=1), "mp")
    cubed = saved_scale * saved_scale * saved_scale
    input_grad = (
        upstream.astype(jnp.float32)
        + saved_scale * scaled_grad
        - saved_values * cubed * (row_dot[:, None] / full_width)
    ).astype(jnp.bfloat16)
    next_input = shifted(output, "section", 1)
    prev_grad = shifted(input_grad, "section", -1)
    down_grad = down_sum / replicas
    up_grad = up_sum / replicas
    return (next_input[None], prev_grad[None], down_grad[None], up_grad[None])


def solution(mesh):
    placed = (
        P("section", "dp", "mp"),
        P("dp"),
        P("mp"),
        P("section", "dp", "mp"),
        P("section", "dp", "mp"),
        P("section", "mp"),
        P("section", None, "mp"),
        P("section", "mp", None),
    )
    return jax.shard_map(
        on_device,
        mesh=mesh,
        in_specs=placed,
        out_specs=(
            P("section", "dp", "mp"),
            P("section", "dp", "mp"),
            P("section", "dp", "mp"),
            P("section", "mp", "dp"),
        ),
        check_vma=False,
    )
```

profile of v0, /device:TPU:24, one launch (start us, length us, event | category | flops | bytes accessed | tf_op | source)
XLA Modules:
  0.0 417.9 jit_solution(1169988477661159644)
XLA Ops:
  7.2 0.8 compare_or_fusion
  8.1 2.4 bitcast_select_fusion
  10.6 0.7 all-gather.9.cloned.1.call-update
  11.3 0.7 all-gather.11.cloned.1.call-update
  12.1 4.4 %all-gather = bf16[1,8192]{1,0:T(2,128)(2,1)S(1)} all-gather(bf16[1,4096]{1,0:T(2,128)(2,1)S(1)} %copy-done.3), channel_id=2, replica_groups=mesh['dp'=4,'section'=4,'mp'=2] {'mp'}, dimensions={1}, use_global_device_ids=true | all-gather | bytes 24576 | tf_op jit(solution)/shard_map/all_gather | solution.py:44
  16.5 31.2 %all-gather.7.cloned.1.call-done = bf16[144,8192]{1,0:T(8,128)(2,1)} async-done(((bf16[144,4096]{1,0:T(8,128)(2,1)}), bf16[144,8192]{1,0:T(8,128)(2,1)}) %all-gather.7.cloned.1.call-update) | async-done | bytes 2359312 | tf_op jit(solution)/shard_map/all_gather | solution.py:41
  47.7 2.2 fusion
  50.0 6.1 %fusion.19 = f32[144,8192]{1,0:T(8,128)} fusion(bf16[1,128,8192]{2,1,0:T(8,128)(2,1)} %param.15, bf16[1,8192,128]{2,1,0:T(8,128)(2,1)S(1)} %copy-done, bf16[144,8192]{1,0:T(8,128)(2,1)} %all-gather.7.cloned.1.call-done, f32[8192]{0:T(1024)S(1)} %bitcast.61, f32[144]{0:T(256)S(1)} %add_rsqrt_fusion.1), kind=kOutput, calls=%fused_computation.26 | convolution fusion | flops 608790528 | bytes 11305536 | tf_op jit(solution)/shard_map/dot_general | solution.py:53
  56.1 0.0 reduce-scatter.7.cloned.1.call-start
  56.1 29.3 %all-gather.9.cloned.1.call-done = bf16[1,144,8192]{2,1,0:T(8,128)(2,1)} async-done(((bf16[1,144,4096]{2,1,0:T(8,128)(2,1)}), bf16[1,144,8192]{2,1,0:T(8,128)(2,1)}) %all-gather.9.cloned.1.call-update) | async-done | bytes 2359312 | tf_op jit(solution)/shard_map/all_gather | solution.py:42
  85.4 2.4 fusion.3
  87.8 1.0 fusion.23
  88.7 34.3 %all-gather.11.cloned.1.call-done = bf16[1,144,8192]{2,1,0:T(8,128)(2,1)} async-done(((bf16[1,144,4096]{2,1,0:T(8,128)(2,1)}), bf16[1,144,8192]{2,1,0:T(8,128)(2,1)}) %all-gather.11.cloned.1.call-update) | async-done | bytes 2359312 | tf_op jit(solution)/shard_map/all_gather | solution.py:43
  123.0 3.1 fusion.36
  126.1 2.9 fusion.21
  129.1 4.5 %fusion.12 = f32[128,8192]{1,0:T(8,128)} fusion(bf16[1,144,8192]{2,1,0:T(8,128)(2,1)} %all-gather.11.cloned.1.call-done, f32[144,128]{1,0:T(8,128)S(1)} %fusion.23), kind=kOutput, calls=%fused_computation.18 | convolution fusion | flops 302082048 | bytes 6627328 | tf_op jit(solution)/shard_map/dot_general | solution.py:19
  133.6 0.0 reduce-scatter.9.cloned.1.call-start
  133.7 5.1 %fusion.41 = f32[8192,128]{1,0:T(8,128)} fusion(bf16[144,128]{1,0:T(8,128)(2,1)S(1)} %fusion.36, bf16[1,144,8192]{2,1,0:T(8,128)(2,1)} %all-gather.9.cloned.1.call-done, f32[144]{0:T(256)S(1)} %get-tuple-element.5, f32[8192]{0:T(1024)S(1)} %bitcast.63), kind=kOutput, calls=%fused_computation.39 | convolution fusion | flops 306708480 | bytes 6623808 | tf_op jit(solution)/shard_map/dot_general | solution.py:19
  138.8 46.4 %reduce-scatter.5.cloned.1.call-done = f32[144,4096]{1,0:T(8,128)} async-done(((f32[144,8192]{1,0:T(8,128)}), f32[144,4096]{1,0:T(8,128)}) %reduce-scatter.5.cloned.1.call-update) | async-done | bytes 2359312 | tf_op jit(solution)/shard_map/reduce_scatter | solution.py:71
  185.2 3.4 add_convert_fusion
  188.6 2.8 collective-permute-start
  191.4 56.2 %reduce-scatter.7.cloned.1.call-done = f32[144,4096]{1,0:T(8,128)} async-done(((f32[144,8192]{1,0:T(8,128)}), f32[144,4096]{1,0:T(8,128)}) %reduce-scatter.7.cloned.1.call-update) | async-done | bytes 2359312 | tf_op jit(solution)/shard_map/reduce_scatter | solution.py:72
  247.5 2.1 fusion.9
  249.6 4.9 %psum.7 = f32[144]{0:T(256)S(1)} all-reduce(f32[144]{0:T(256)S(1)} %fusion.9), channel_id=1, replica_groups=mesh['dp'=4,'section'=4,'mp'=2] {'mp'}, use_global_device_ids=true, to_apply=%region_5.6 | all-reduce | flops 144 | bytes 1152 | tf_op jit(solution)/shard_map/psum | solution.py:77
  254.5 4.6 %fusion.8 = bf16[144,4096]{1,0:T(8,128)(2,1)} fusion(f32[144,4096]{1,0:T(8,128)} %reduce-scatter.7.cloned.1.call-done, bf16[1,144,4096]{2,1,0:T(8,128)(2,1)} %param.12, bf16[1,144,4096]{2,1,0:T(8,128)(2,1)S(1)} %copy-done.2, f32[144]{0:T(256)S(1)} %broadcast_multiply_fusion, f32[144]{0:T(256)S(1)} %get-tuple-element.4, f32[4096]{0:T(1024)S(1)} %bitcast.65, ...), kind=kLoop, calls=%fused_computation.14 | loop fusion | flops 5308416 | bytes 5916352 | tf_op jit(solution)/shard_map/convert_element_type | solution.py:83
  259.1 1.3 collective-permute-start.1
  260.4 65.3 %reduce-scatter.11.cloned.1.call-done = f32[128,2048]{1,0:T(8,128)} async-done(((f32[128,8192]{1,0:T(8,128)}), f32[128,2048]{1,0:T(8,128)}) %reduce-scatter.11.cloned.1.call-update) | async-done | bytes 1048592 | tf_op jit(solution)/shard_map/reduce_scatter | solution.py:68
  325.7 2.3 multiply_bitcast_fusion
  328.0 77.4 %reduce-scatter.9.cloned.1.call-done = f32[2048,128]{1,0:T(8,128)} async-done(((f32[8192,128]{1,0:T(8,128)}), f32[2048,128]{1,0:T(8,128)}) %reduce-scatter.9.cloned.1.call-update) | async-done | bytes 1048592 | tf_op jit(solution)/shard_map/reduce_scatter | solution.py:67
  405.4 2.3 multiply_bitcast_fusion.1
  407.7 2.4 copy.14
  410.0 1.0 copy.15
  (27 shorter events, 0.4 us)
Async XLA Ops:
  7.2 42.8 %copy-start = (bf16[1,8192,128]{2,1,0:T(8,128)(2,1)S(1)}, bf16[1,8192,128]{2,1,0:T(8,128)(2,1)}, u32[]{:S(2)}) copy-start(bf16[1,8192,128]{2,1,0:T(8,128)(2,1)} %param.14) | copy-start | bytes 6291460
  7.2 40.5 %all-gather.7.cloned.1.call-start = ((), (), s32[]{:S(2)}) async-start(), calls=%async_computation.4 | async-start | bytes 3538944 | tf_op jit(solution)/shard_map/all_gather | solution.py:41
  10.5 1.6 copy-start.3
  10.5 74.9 %all-gather.9.cloned.1.call-start = ((), (), s32[]{:S(2)}) async-start(), calls=%async_computation.9 | async-start | bytes 3538944 | tf_op jit(solution)/shard_map/all_gather | solution.py:42
  11.3 111.8 %all-gather.11.cloned.1.call-start = ((), (), s32[]{:S(2)}) async-start(), calls=%async_computation.10 | async-start | bytes 3538944 | tf_op jit(solution)/shard_map/all_gather | solution.py:43
  12.0 173.2 %reduce-scatter.5.cloned.1.call-start = ((), (), s32[]{:S(2)}) async-start(), calls=%async_computation.5 | async-start | bytes 7077888 | tf_op jit(solution)/shard_map/reduce_scatter | solution.py:71
  56.1 191.4 %reduce-scatter.7.cloned.1.call-start = ((), (), s32[]{:S(2)}) async-start(), calls=%async_computation.6 | async-start | bytes 7077888 | tf_op jit(solution)/shard_map/reduce_scatter | solution.py:72
  85.4 2.4 copy-start.1
  129.1 196.6 %reduce-scatter.11.cloned.1.call-start = ((), (), s32[]{:S(2)}) async-start(), calls=%async_computation.8 | async-start | bytes 5242880 | tf_op jit(solution)/shard_map/reduce_scatter | solution.py:68
  133.6 271.7 %reduce-scatter.9.cloned.1.call-start = ((), (), s32[]{:S(2)}) async-start(), calls=%async_computation.7 | async-start | bytes 5242880 | tf_op jit(solution)/shard_map/reduce_scatter | solution.py:67
  138.8 46.5 %copy-start.4 = (bf16[4096]{0:T(1024)(128)(2,1)S(1)}, bf16[4096]{0:T(1024)(128)(2,1)}, u32[]{:S(2)}) copy-start(bf16[4096]{0:T(1024)(128)(2,1)} %param.10) | copy-start | bytes 24580
  138.8 108.7 %copy-start.2 = (bf16[1,144,4096]{2,1,0:T(8,128)(2,1)S(1)}, bf16[1,144,4096]{2,1,0:T(8,128)(2,1)}, u32[]{:S(2)}) copy-start(bf16[1,144,4096]{2,1,0:T(8,128)(2,1)} %param.11) | copy-start | bytes 3538948
  188.6 219.1 %collective-permute-start = (bf16[144,4096]{1,0:T(8,128)(2,1)}, bf16[144,4096]{1,0:T(8,128)(2,1)}, u32[]{:S(2)}, u32[]{:S(2)}) collective-permute-start(bf16[144,4096]{1,0:T(8,128)(2,1)} %add_convert_fusion), channel_id=1, source_target_pairs={{0,2},{2,4},{4,6},{1,3},{3,5},{5,7},{8,10},{10,12},{12,14},{9,11},... | collective-permute-start | bytes 3538952 | tf_op jit(solution)/shard_map/ppermute | solution.py:10
  259.1 148.6 %collective-permute-start.1 = (bf16[144,4096]{1,0:T(8,128)(2,1)}, bf16[144,4096]{1,0:T(8,128)(2,1)S(1)}, u32[]{:S(2)}, u32[]{:S(2)}) collective-permute-start(bf16[144,4096]{1,0:T(8,128)(2,1)} %fusion.8), channel_id=1, source_target_pairs={{2,0},{4,2},{6,4},{3,1},{5,3},{7,5},{10,8},{12,10},{14,12},{11,9},... | collective-permute-start | bytes 3538952 | tf_op jit(solution)/shard_map/ppermute | solution.py:10
Sparse Core Ops, SparseCore 0:
  10.6 37.0 all-gather.6
  49.3 36.0 all-gather.8
  86.9 36.0 all-gather.10
  125.2 59.9 reduce-scatter.4
  187.5 59.9 reduce-scatter.6
  249.7 75.9 reduce-scatter.10
  328.1 77.2 reduce-scatter.8
where the time goes:
time: 421 us; the launch traced here: 418 us
  waiting for transfers between devices  342 us (81%)
  matrix products  22.6 us (5%)
  other arithmetic  22.5 us (5%)
  between operations  14.2 us (3%)
  blocking collectives  9.35 us (2%)
  starting transfers between devices  4.31 us (1%)
    reduce_scatter x1, waiting for transfers between devices, on_device(): lax.psum_scatter(down_part, 'dp', scatter_dimension=0, tiled=True)  77.4 us
    reduce_scatter x1, waiting for transfers between devices, on_device(): lax.psum_scatter(up_part, 'dp', scatter_dimension=1, tiled=True)  65.3 us
    reduce_scatter x1, waiting for transfers between devices, on_device(): lax.psum_scatter(normed_part, 'mp', scatter_dimension=1, tiled=True)  56.2 us
    reduce_scatter x1, waiting for transfers between devices, on_device(): lax.psum_scatter(branch_part, 'mp', scatter_dimension=1, tiled=True)  46.4 us
    all_gather x1, waiting for transfers between devices, on_device(): lax.all_gather(upstream, 'mp', axis=1, tiled=True)  34.3 us
    all_gather x1, waiting for transfers between devices, on_device(): lax.all_gather(inputs, 'mp', axis=1, tiled=True)  31.2 us
    all_gather x1, waiting for transfers between devices, on_device(): lax.all_gather(saved, 'mp', axis=1, tiled=True)  29.3 us
    dot_general x2, matrix products, contract_rows(): lax.dot_general(left, right, (((0,), (0,)), ((), ())), preferred_element_...  9.56 us
  transfers between devices with their start and end apart: 9, of which 7 were waited for; matrix products, arithmetic and copies ran while one was open for 10% of the time, Pallas kernels for 0%

commit v1 on v0

v1 whole, which is shorter than its diff:
```python
import functools

import jax
import jax.numpy as jnp
from jax import lax
from jax.experimental import pallas as pl
from jax.experimental.pallas import tpu as pltpu
from jax.sharding import PartitionSpec as P

F32 = jnp.float32
BF16 = jnp.bfloat16
MESH = pl.DeviceIdType.MESH


def dot(left, right, dims):
    return lax.dot_general(left, right, (dims, ((), ())), preferred_element_type=F32)


def kernel(
    sizes,
    arr, keep, maskv, sta, cot, gain, down, up,
    nxt, prv, dgo, ugo,
    wd, wu, xin, normed, scaled, acts, pg, sc_all, nall,
    ss_loc, ss_rem, g_own, g_rem, part, part_rem, rd_loc, rd_rem, out_st, grad_st, res_d, res_u,
    w_ssem, w_rsem, w_lsem, g_ssem, g_rsem, ss_ssem, ss_rsem, a_ssem, a_rsem, a_lsem,
    p_ssem, p_rsem, pg_ssem, pg_rsem, sc_ssem, sc_rsem, rd_ssem, rd_rsem,
    o_ssem, o_rsem, r_ssem, r_rsem,
):
    Z, S, rows, half, units = sizes
    H = Z // 2
    full = 2 * half
    F = full // (2 * Z)
    C = min(half, 512)
    chunks = half // C
    d = lax.axis_index("dp")
    s = lax.axis_index("section")
    m = lax.axis_index("mp")
    om = 1 - m
    peer = (d, s, om)

    def rcopy(src, dst, ssem, rsem, dev):
        return pltpu.make_async_remote_copy(
            src_ref=src, dst_ref=dst, send_sem=ssem, recv_sem=rsem,
            device_id=dev, device_id_type=MESH,
        )

    barrier = pltpu.get_barrier_semaphore()

    @pl.loop(0, Z)
    def _(i):
        pl.semaphore_signal(barrier, inc=1, device_id=(i, s, om), device_id_type=MESH)

    @pl.loop(1, Z)
    def _(i):
        pl.semaphore_signal(
            barrier, inc=1, device_id=(lax.rem(d + i, Z), s, m), device_id_type=MESH
        )

    @pl.when(s > 0)
    def _():
        pl.semaphore_signal(barrier, inc=1, device_id=(d, s - 1, m), device_id_type=MESH)

    @pl.when(s < S - 1)
    def _():
        pl.semaphore_signal(barrier, inc=1, device_id=(d, s + 1, m), device_id_type=MESH)

    @pl.when(jnp.logical_and(s > 0, s < S - 1))
    def _():
        pl.semaphore_wait(barrier, 2 * Z + 1)

    @pl.when(jnp.logical_or(s == 0, s == S - 1))
    def _():
        pl.semaphore_wait(barrier, 2 * Z)

    mine = pl.multiple_of(m * half, half)
    other = pl.multiple_of(om * half, half)
    send_up = rcopy(up.at[:, pl.ds(other, half)], wu.at[pl.ds(units, units), :],
                    w_ssem.at[0], w_rsem.at[0], peer)
    send_down = rcopy(down.at[pl.ds(other, half), :], wd.at[:, pl.ds(units, units)],
                      w_ssem.at[1], w_rsem.at[1], peer)
    send_up.start()
    send_down.start()
    own_up = pltpu.make_async_copy(up.at[:, pl.ds(mine, half)], wu.at[pl.ds(0, units), :], w_lsem.at[0])
    own_down = pltpu.make_async_copy(down.at[pl.ds(mine, half), :], wd.at[:, pl.ds(0, units)], w_lsem.at[1])
    own_up.start()
    own_down.start()

    def act_copy(a, src, j, mt):
        col = pl.multiple_of((j * 2 + mt) * F, F)
        to = m * H + j
        return rcopy(src.at[:, pl.ds(col, F)], acts.at[a, d], a_ssem.at[a, j * 2 + mt],
                     a_rsem.at[a, d], (to, s, mt))

    def act_own(a, src):
        col = pl.multiple_of(((d - m * H) * 2 + m) * F, F)
        return pltpu.make_async_copy(src.at[:, pl.ds(col, F)], acts.at[a, d], a_lsem.at[a])

    keeps_own = (d // H) == m

    def plane_sends(go, a, src):
        @pl.loop(0, H)
        def _(j):
            @pl.when(m * H + j != d)
            def _():
                go(act_copy(a, src, j, m))

    def cross_sends(go, a, src):
        @pl.loop(0, H)
        def _(j):
            go(act_copy(a, src, j, om))

    for a, src in ((0, sta), (1, cot)):
        plane_sends(lambda c: c.start(), a, src)

        @pl.when(keeps_own)
        def _():
            act_own(a, src).start()

    g_own[...] = gain[...].astype(F32)
    gain_copy = rcopy(g_own, g_rem, g_ssem, g_rsem, peer)
    gain_copy.start()

    keep_row = jnp.logical_or(keep[...] == 1, s != 0)

    def at(i, size=C):
        return pl.ds(pl.multiple_of(i * size, size), size)

    def fold(v):
        total = v[:, :128]
        for k in range(1, v.shape[1] // 128):
            total = total + v[:, 128 * k:128 * (k + 1)]
        return total

    def squares(i, carry):
        cx, cs = carry
        v = jnp.where(keep_row, arr[:, at(i)].astype(F32), maskv[:, at(i)].astype(F32))
        xin[:, at(i)] = v.astype(BF16)
        w = sta[:, at(i)].astype(F32)
        return cx + fold(v * v), cs + fold(w * w)

    zero = jnp.zeros((rows, 128), F32)
    cx, cs = lax.fori_loop(0, chunks, squares, (zero, zero))
    lane = lax.broadcasted_iota(jnp.int32, (rows, 128), 1)
    ss_loc[...] = jnp.where(
        lane < 64, jnp.sum(cx, axis=1, keepdims=True), jnp.sum(cs, axis=1, keepdims=True)
    )
    ss_copy = rcopy(ss_loc, ss_rem, ss_ssem, ss_rsem, peer)
    ss_copy.start()

    def part_copy(k):
        return rcopy(part.at[k], part_rem.at[k], p_ssem.at[k], p_rsem.at[k], peer)

    acc0 = jnp.zeros((rows, 2 * units), F32)
    own_up.wait()
    send_up.wait_recv()
    part[0] = lax.fori_loop(
        0, chunks, lambda i, acc: acc + dot(cot[:, at(i)], wu[:, at(i)], ((1,), (1,))), acc0
    )
    part_copy(0).start()

    ss_copy.wait_recv()
    total = (ss_loc[...] + ss_rem[...]) / full
    scales = lax.rsqrt(total + 1e-05)
    scale_f = scales[:, 0:1]
    scale_b = scales[:, 127:128]
    sc_all[d] = jnp.broadcast_to(scale_b, (rows, 128))

    def sc_copy(i):
        return rcopy(sc_all.at[d], sc_all.at[d], sc_ssem.at[i], sc_rsem.at[d],
                     (lax.rem(d + i, Z), s, m))

    @pl.loop(1, Z)
    def _(i):
        sc_copy(i).start()

    def normalise(k, src, scale):
        @pl.loop(0, chunks)
        def _(i):
            normed[k, :, at(i)] = (
                src[:, at(i)].astype(F32) * scale * g_own[:, at(i)]
            ).astype(BF16)

    normalise(0, sta, scale_b)
    normalise(1, xin, scale_f)
    own_down.wait()
    send_down.wait_recv()
    for k in (0, 1):
        part[1 + k] = lax.fori_loop(
            0, chunks, lambda i, acc: acc + dot(normed[k, :, at(i)], wd[at(i), :], ((1,), (0,))), acc0
        )
        part_copy(1 + k).start()

    send_up.wait_send()
    send_down.wait_send()
    for a, src in ((0, sta), (1, cot)):
        cross_sends(lambda c: c.start(), a, src)

    def whole_sum(k):
        part_copy(k).wait_recv()
        return jnp.concatenate(
            [part[k, :, :units] + part_rem[k, :, units:], part[k, :, units:] + part_rem[k, :, :units]],
            axis=1,
        )

    hidden_grad = whole_sum(0)
    saved_pre = whole_sum(1)
    sigma = jax.nn.sigmoid(saved_pre)
    pre_grad = (hidden_grad * sigma * (1.0 + saved_pre * (1.0 - sigma))).astype(BF16)
    pg[d, :, :2 * units] = pre_grad
    pg[d, :, 2 * units:] = (saved_pre * sigma).astype(BF16)

    def pg_copy(i):
        return rcopy(pg.at[d], pg.at[d], pg_ssem.at[i], pg_rsem.at[d],
                     (lax.rem(d + i, Z), s, m))

    @pl.loop(1, Z)
    def _(i):
        pg_copy(i).start()

    def grads(i, acc):
        v = dot(pre_grad, wd[at(i), :], ((1,), (1,))) * g_own[:, at(i)]
        scaled[:, at(i)] = v
        return acc + fold(v * sta[:, at(i)].astype(F32))

    rdot = lax.fori_loop(0, chunks, grads, zero)
    rd_loc[...] = jnp.broadcast_to(jnp.sum(rdot, axis=1, keepdims=True), (rows, 128))
    rd_copy = rcopy(rd_loc, rd_rem, rd_ssem, rd_rsem, peer)
    rd_copy.start()

    pre = whole_sum(2)
    hidden = (pre * jax.nn.sigmoid(pre)).astype(BF16)

    @pl.loop(0, chunks)
    def _(i):
        out_st[:, at(i)] = (
            xin[:, at(i)].astype(F32) + dot(hidden, wu[:, at(i)], ((1,), (0,)))
        ).astype(BF16)

    def out_copy():
        return rcopy(out_st, nxt, o_ssem.at[0], o_rsem.at[0], (d, s + 1, m))

    def grad_copy():
        return rcopy(grad_st, prv, o_ssem.at[1], o_rsem.at[1], (d, s - 1, m))

    @pl.when(s < S - 1)
    def _():
        out_copy().start()

    rd_copy.wait_recv()
    row_dot = (rd_loc[...] + rd_rem[...])[:, 0:1]
    back = scale_b * scale_b * scale_b * (row_dot / full)

    @pl.loop(0, chunks)
    def _(i):
        grad_st[:, at(i)] = (
            cot[:, at(i)].astype(F32) + scale_b * scaled[:, at(i)] - sta[:, at(i)].astype(F32) * back
        ).astype(BF16)

    @pl.when(s > 0)
    def _():
        grad_copy().start()

    @pl.when(s == 0)
    def _():
        nxt[...] = jnp.zeros_like(nxt)

    @pl.when(s == S - 1)
    def _():
        prv[...] = jnp.zeros_like(prv)

    gain_copy.wait_recv()
    FC = min(F, 512)
    slice_half = d // H
    gcol = pl.multiple_of(((d - slice_half * H) * 2 + m) * F, F)

    def wait_act(a, i):
        local = jnp.logical_and(i == d, keeps_own)

        @pl.when(local)
        def _():
            act_own(a, sta if a == 0 else cot).wait()

        @pl.when(jnp.logical_not(local))
        def _():
            rcopy(acts.at[a, i], acts.at[a, i], a_ssem.at[a, 0], a_rsem.at[a, i], peer).wait_recv()

    @pl.loop(0, Z)
    def _(i):
        wait_act(1, i)

        @pl.when(i != d)
        def _():
            rcopy(pg.at[i], pg.at[i], pg_ssem.at[0], pg_rsem.at[i], peer).wait_recv()
            rcopy(sc_all.at[i], sc_all.at[i], sc_ssem.at[0], sc_rsem.at[i], peer).wait_recv()

    def res_copy(k):
        if k == 0:
            return rcopy(res_u, ugo.at[:, pl.ds(pl.multiple_of(m * F, F), F)],
                         r_ssem.at[0], r_rsem.at[0], peer)
        return rcopy(res_d, dgo.at[pl.ds(pl.multiple_of(m * F, F), F), :],
                     r_ssem.at[1], r_rsem.at[1], peer)

    tokens = Z * rows
    hid_all = pg[:, :, 2 * units:].reshape(tokens, 2 * units)
    for c in range(F // FC):
        cols = slice(c * FC, (c + 1) * FC)
        got = dot(hid_all, acts[1, :, :, cols].reshape(tokens, FC), ((0,), (0,))) / Z
        ugo[:, pl.ds(pl.multiple_of(m * F + c * FC, FC), FC)] = got[:units]
        res_u[:, cols] = got[units:]
    res_copy(0).start()

    @pl.loop(0, Z)
    def _(i):
        wait_act(0, i)
        g = jnp.where(slice_half == m, g_own[:, pl.ds(gcol, F)], g_rem[:, pl.ds(gcol, F)])
        nall[i] = (acts[0, i].astype(F32) * sc_all[i][:, 0:1] * g).astype(BF16)

    pg_all = pg[:, :, :2 * units].reshape(tokens, 2 * units)
    for c in range(F // FC):
        cols = slice(c * FC, (c + 1) * FC)
        got = dot(nall[:, :, cols].reshape(tokens, FC), pg_all, ((0,), (0,))) / Z
        dgo[pl.ds(pl.multiple_of(m * F + c * FC, FC), FC), :] = got[:, :units]
        res_d[cols, :] = got[:, units:]
    res_copy(1).start()

    for a, src in ((0, sta), (1, cot)):
        plane_sends(lambda c: c.wait_send(), a, src)
        cross_sends(lambda c: c.wait_send(), a, src)
    gain_copy.wait_send()
    ss_copy.wait_send()
    rd_copy.wait_send()
    for k in range(3):
        part_copy(k).wait_send()

    @pl.loop(1, Z)
    def _(i):
        sc_copy(i).wait_send()
        pg_copy(i).wait_send()

    @pl.when(s < S - 1)
    def _():
        out_copy().wait_send()
        grad_copy().wait_recv()

    @pl.when(s > 0)
    def _():
        out_copy().wait_recv()
        grad_copy().wait_send()

    res_copy(0).wait()
    res_copy(1).wait()


def on_device(Z, S, arriving, keep_mask, mask_vector, stashed, cotangent, gain, down_adapter, up_adapter):
    _, rows, half = arriving.shape
    units = up_adapter.shape[1]
    F = half // Z
    full = 2 * half
    vm = pl.BlockSpec(memory_space=pltpu.VMEM)
    hbm = pl.BlockSpec(memory_space=pl.ANY)
    dma = pltpu.SemaphoreType.DMA
    vmem = pltpu.VMEM
    nxt, prv, dgo, ugo = pl.pallas_call(
        functools.partial(kernel, (Z, S, rows, half, units)),
        out_shape=(
            jax.ShapeDtypeStruct((rows, half), BF16),
            jax.ShapeDtypeStruct((rows, half), BF16),
            jax.ShapeDtypeStruct((full // Z, units), F32),
            jax.ShapeDtypeStruct((units, full // Z), F32),
        ),
        in_specs=[vm] * 6 + [hbm] * 2,
        out_specs=(vm,) * 4,
        scratch_shapes=[
            vmem((half, 2 * units), BF16),
            vmem((2 * units, half), BF16),
            vmem((rows, half), BF16),
            vmem((2, rows, half), BF16),
            vmem((rows, half), F32),
            vmem((2, Z, rows, F), BF16),
            vmem((Z, rows, 4 * units), BF16),
            vmem((Z, rows, 128), F32),
            vmem((Z, rows, F), BF16),
            vmem((rows, 128), F32),
            vmem((rows, 128), F32),
            vmem((1, half), F32),
            vmem((1, half), F32),
            vmem((3, rows, 2 * units), F32),
            vmem((3, rows, 2 * units), F32),
            vmem((rows, 128), F32),
            vmem((rows, 128), F32),
            vmem((rows, half), BF16),
            vmem((rows, half), BF16),
            vmem((F, units), F32),
            vmem((units, F), F32),
            dma((2,)), dma((2,)), dma((2,)), dma, dma, dma, dma,
            dma((2, Z)), dma((2, Z)), dma((2,)),
            dma((3,)), dma((3,)), dma((Z,)), dma((Z,)), dma((Z,)), dma((Z,)), dma, dma,
            dma((2,)), dma((2,)), dma((2,)), dma((2,)),
        ],
        compiler_params=pltpu.CompilerParams(
            collective_id=0, has_side_effects=True, vmem_limit_bytes=56 * 1024 * 1024
        ),
    )(
        arriving[0], keep_mask[:, None], mask_vector[None], stashed[0], cotangent[0],
        gain, down_adapter[0], up_adapter[0],
    )
    return nxt[None], prv[None], dgo[None], ugo[None]


def solution(mesh):
    return jax.shard_map(
        functools.partial(on_device, mesh.shape["dp"], mesh.shape["section"]),
        mesh=mesh,
        in_specs=(
            P("section", "dp", "mp"),
            P("dp"),
            P("mp"),
            P("section", "dp", "mp"),
            P("section", "dp", "mp"),
            P("section", "mp"),
            P("section", None, "mp"),
            P("section", "mp", None),
        ),
        out_specs=(
            P("section", "dp", "mp"),
            P("section", "dp", "mp"),
            P("section", "dp", "mp"),
            P("section", "mp", "dp"),
        ),
        check_vma=False,
    )
```

time: 421 us -> 166 us (0.39)
  waiting for transfers between devices: 342 us -> 0 us
  Pallas kernels: 0 us -> 156 us
  matrix products: 22.6 us -> 0 us
  other arithmetic: 22.5 us -> 0 us
  between operations: 14.2 us -> 0.65 us
  blocking collectives: 9.35 us -> 0 us
  local copies, waits for them, and re-layouts: 3.43 us -> 9.44 us
  starting transfers between devices: 4.31 us -> 0 us
    reduce_scatter x4 -> x0, waiting for transfers between devices: 245 us -> none  [the longest x1 77.4 us: on_device(): lax.psum_scatter(down_part, 'dp', scatter_dimension=0, tiled=True)]
    pallas_call x0 -> x1, Pallas kernels: none -> 156 us  [on_device(): pl.pallas_call(functools.partial(kernel, (Z, S, rows, half, units)), out_...]
    all_gather x3 -> x0, waiting for transfers between devices: 94.8 us -> none  [the longest x1 34.3 us: on_device(): lax.all_gather(upstream, 'mp', axis=1, tiled=True)]
    dot_general x6 -> x0, matrix products: 22.6 us -> none  [the longest x2 9.56 us: contract_rows(): lax.dot_general(left, right, (((0,), (0,)), ((), ())), preferred_element_...]
    convert_element_type x3 -> x0, other arithmetic: 7.97 us -> none  [the longest x1 4.55 us: on_device(): input_grad = (upstream.astype(jnp.float32) + saved_scale * scaled_grad -...]
    reduce_sum x3 -> x0, other arithmetic: 6.67 us -> none  [the longest x2 4.61 us: row_scale(): return lax.rsqrt(jnp.mean(values * values, axis=1, keepdims=True) + 1e-05)]
    psum x1 -> x0, blocking collectives: 4.93 us -> none  [on_device(): row_dot = lax.psum(jnp.sum(saved_values * scaled_grad, axis=1), 'mp')]
    broadcast_in_dim x2 -> x0, other arithmetic: 4.55 us -> none  [on_device(): return (next_input[None], prev_grad[None], down_grad[None], up_grad[None])]
  transfers between devices with their start and end apart: 9 -> 0, of which waited for: 7 -> 0; matrix products, arithmetic and copies ran while one was open for 10% -> 0% of each run, Pallas kernels for 0% -> 0%
where the time goes in v1:
time: 166 us
  Pallas kernels  156 us (94%)
  local copies, waits for them, and re-layouts  9.44 us (6%)
    pallas_call x1, Pallas kernels, on_device(): pl.pallas_call(functools.partial(kernel, (Z, S, rows, half, units)), out_...  156 us
    unnamed x10, local copies, waits for them, and re-layouts  6.71 us

profile of v1, /device:TPU:24, one launch (start us, length us, event | category | flops | bytes accessed | tf_op | source)
XLA Modules:
  0.0 165.9 jit_solution(15196320589930016715)
XLA Ops:
  0.6 1.3 broadcast_in_dim.19.maskv
  1.9 1.4 copy.12.keep
  3.4 155.8 %shard_map.111 = (bf16[144,4096]{1,0:T(8,128)(2,1)}, bf16[144,4096]{1,0:T(8,128)(2,1)}, f32[2048,128]{1,0:T(8,128)}, f32[128,2048]{1,0:T(8,128)}) custom-call(bf16[144,4096]{1,0:T(8,128)(2,1)} %bitcast.14, s32[144,1]{1,0:T(8,128)} %copy.12.keep, bf16[1,4096]{1,0:T(2,128)(2,1)} %broadcast_in_dim.19.maskv, bf16[144,4096]{1,0:T(8,128)(2,1)} %bitcast.15, ...), custom_call_target="tpu_custom_call" | custom-call | tf_op jit(solution)/shard_map/pallas_call | solution.py:363
  159.2 0.0 copy-start
  159.2 2.5 %copy.17 = bf16[1,144,4096]{2,1,0:T(8,128)(2,1)} copy(bf16[1,144,4096]{2,1,0:T(8,128)(2,1)} %bitcast.13) | data formatting | bytes 2359296
  161.7 0.0 copy-done
  161.7 0.0 copy-start.2
  161.7 1.0 copy.18
  162.7 0.6 copy-done.2
  163.4 0.0 copy-start.1
  163.4 1.0 copy.19
  164.3 0.6 copy-done.1
  165.0 1.0 copy.20
Async XLA Ops:
  159.2 2.5 %copy-start = (bf16[144,4096]{1,0:T(8,128)(2,1)S(1)}, bf16[144,4096]{1,0:T(8,128)(2,1)}, u32[]{:S(2)}) copy-start(bf16[144,4096]{1,0:T(8,128)(2,1)} %get-tuple-element.9) | copy-start | bytes 3538948
  161.7 1.7 copy-start.2
  163.4 1.6 copy-start.1
